TPU v7x, 32 devices: a whole 2x2x4 slice. The times are simulated.
32 devices in a mesh: rows: 2 (over core), trans: 8 (over z, x), gvec: 2 (over y).
Axes of the slice: x: 2, y: 2, z: 4, core: 2. Of those that a mesh axis runs over, the one named last changes fastest.
Arguments:
- pair_density: bfloat16 [2, 8192, 4096], P(None, 'trans', 'gvec'), may hold values from -0.75 to 0.75
- coulomb: float32 [4096], P('gvec'), may hold values from 0.1 to 10
- block_index: int32 [2], P('rows'), parts along dimension 0, may hold values from 0 to 7
Outputs:
- kernel_rows: bfloat16 [2, 2048, 8192], P(None, ('rows', 'gvec'), 'trans'), parts along dimension 1
- mirrored: bfloat16 [2, 8192, 2048], P(None, 'trans', 'rows'), parts along dimension 2
There are 2 independent parts, one for each index of `rows`. A program takes and returns all parts, laid end to end along the dimension named above; an argument that names none is the same for every part. Nothing has to cross between parts.
All inputs are finite; a program needn't handle non-finite values.
Results may differ from a plain program's by a relative error of at most 0.017.
Values may be sent and summed in bfloat16 or wider, within the bound.
A program may use at most 64 MiB of HBM per device.

v0:
```python
import jax
import jax.numpy as jnp
from jax import lax
from jax.sharding import PartitionSpec as P


def from_root(value, axis, source):
    kept = jnp.where(lax.axis_index(axis) == source, value, 0).astype(value.dtype)
    return lax.psum(kept, axis)


def contract(left, right):
    return lax.dot_general(
        left, right, (((1,), (1,)), ((), ())), preferred_element_type=jnp.float32
    )


def body(pair_density, coulomb, block_index):
    block = from_root(pair_density, "trans", block_index[0])
    weighted = (block.astype(jnp.float32) * coulomb[None, None, :]).astype(jnp.bfloat16)
    real_part = contract(weighted[0], pair_density[0]) + contract(weighted[1], pair_density[1])
    imag_part = contract(weighted[0], pair_density[1]) - contract(weighted[1], pair_density[0])
    partial_terms = jnp.stack([real_part, imag_part])
    kernel_rows = lax.psum_scatter(
        partial_terms.astype(jnp.bfloat16), "gvec", scatter_dimension=1, tiled=True
    )
    gathered = lax.all_gather(kernel_rows, "gvec", axis=1, tiled=True)
    mirrored = jnp.stack([gathered[0].T, -gathered[1].T])
    return (kernel_rows, mirrored)


def solution(mesh):
    placed = (P(None, "trans", "gvec"), P("gvec"), P("rows"))
    return jax.shard_map(
        body,
        mesh=mesh,
        in_specs=placed,
        out_specs=(P(None, ("rows", "gvec"), "trans"), P(None, "trans", "rows")),
        check_vma=False,
    )
```

profile of v0, /device:TPU:18, one launch (start us, length us, event | category | flops | bytes accessed | tf_op | source)
XLA Modules:
  0.0 451.4 jit_solution(1677788747665492417)
XLA Ops:
  7.2 0.0 all-reduce.2.cloned.1.call-start
  7.9 3.8 broadcast_select_fusion
  11.7 0.0 copy-start.1
  11.7 0.0 all-reduce.2.cloned.1.call-update
  11.7 0.0 reduce-scatter.2.cloned.1.call-start
  11.7 271.5 %all-reduce.2.cloned.1.call-done = bf16[2,1024,2048]{2,1,0:T(8,128)(2,1)} async-done(((bf16[2,1024,2048]{2,1,0:T(8,128)(2,1)}), bf16[2,1024,2048]{2,1,0:T(8,128)(2,1)}) %all-reduce.2.cloned.1.call-update) | async-done | bytes 8388624 | tf_op jit(solution)/shard_map/psum | solution.py:9
  283.2 0.0 copy-done.1
  283.2 0.0 slice-start
  283.2 9.9 %multiply_convert_fusion = bf16[2,1024,2048]{2,1,0:T(8,128)(2,1)} fusion(bf16[2,1024,2048]{2,1,0:T(8,128)(2,1)} %all-reduce.2.cloned.1.call-done, f32[2048]{0:T(1024)S(1)} %copy-done.1), kind=kLoop, calls=%fused_computation | loop fusion | flops 12582912 | bytes 16785408 | tf_op jit(solution)/shard_map/convert_element_type | solution.py:20
  293.1 0.0 slice-start.1
  293.1 0.0 copy-start
  293.1 7.7 %fusion = f32[1024,1024]{1,0:T(8,128)S(1)} fusion(bf16[2,1024,2048]{2,1,0:T(8,128)(2,1)} %multiply_convert_fusion, bf16[2,1024,2048]{2,1,0:T(8,128)(2,1)} %param.3), kind=kOutput, calls=%fused_computation.6 | convolution fusion | flops 4294967296 | bytes 12582912 | tf_op jit(solution)/shard_map/dot_general | solution.py:13
  300.8 0.0 slice-done
  300.8 0.0 slice-done.1
  300.8 0.0 copy-done
  300.9 6.1 %fusion.2 = f32[1024,1024]{1,0:T(8,128)} fusion(bf16[2,1024,2048]{2,1,0:T(8,128)(2,1)S(1)} %copy-done, bf16[2,1024,2048]{2,1,0:T(8,128)(2,1)S(1)} %bitcast.45), kind=kOutput, calls=%fused_computation.8 | convolution fusion | flops 4294967296 | bytes 12582912 | tf_op jit(solution)/shard_map/dot_general | solution.py:13
  306.9 4.7 %fusion.13 = bf16[1,1024,1024]{2,1,0:T(8,128)(2,1)S(1)} fusion(f32[1024,1024]{1,0:T(8,128)S(1)} %fusion, bf16[2,1024,2048]{2,1,0:T(8,128)(2,1)S(1)} %bitcast.45, bf16[2,1024,2048]{2,1,0:T(8,128)(2,1)S(1)} %copy-done), kind=kOutput, calls=%fused_computation.21 | convolution fusion | flops 4297064448 | bytes 14680064 | tf_op jit(solution)/shard_map/dot_general | solution.py:13
  311.7 6.3 %fusion.12 = bf16[1,1024,1024]{2,1,0:T(8,128)(2,1)S(1)} fusion(f32[1024,1024]{1,0:T(8,128)} %fusion.2, bf16[2,1024,2048]{2,1,0:T(8,128)(2,1)S(1)} %bitcast.45, bf16[2,1024,2048]{2,1,0:T(8,128)(2,1)S(1)} %copy-done), kind=kOutput, calls=%fused_computation.20 | convolution fusion | flops 4297064448 | bytes 14680064 | tf_op jit(solution)/shard_map/dot_general | solution.py:13
  318.0 2.4 pad_maximum_fusion
  320.4 0.0 reduce-scatter.2.cloned.1.call-update
  320.4 0.0 all-gather.2.cloned.1.call-start
  320.5 54.4 %reduce-scatter.2.cloned.1.call-done = bf16[2,512,1024]{2,1,0:T(8,128)(2,1)} async-done(((bf16[2,1024,1024]{2,1,0:T(8,128)(2,1)}), bf16[2,512,1024]{2,1,0:T(8,128)(2,1)}) %reduce-scatter.2.cloned.1.call-update) | async-done | bytes 2097168 | tf_op jit(solution)/shard_map/reduce_scatter | solution.py:24
  374.9 0.0 all-gather.2.cloned.1.call-update
  374.9 59.0 %all-gather.2.cloned.1.call-done = bf16[2,1024,1024]{2,1,0:T(8,128)(2,1)} async-done(((bf16[2,512,1024]{2,1,0:T(8,128)(2,1)}), bf16[2,1024,1024]{2,1,0:T(8,128)(2,1)}) %all-gather.2.cloned.1.call-update) | async-done | bytes 4194320 | tf_op jit(solution)/shard_map/all_gather | solution.py:27
  433.9 2.5 slice_bitcast_fusion.6
  436.4 2.3 pad_maximum_fusion.1
  438.7 6.2 %copy.5 = bf16[2,1024,1024]{2,1,0:T(8,128)(2,1)} copy(bf16[2,1024,1024]{1,2,0:T(8,128)(2,1)} %pad_maximum_fusion.1) | data formatting | bytes 8388608
  (1 shorter events, 0.0 us)
Async XLA Ops:
  7.2 276.0 %all-reduce.2.cloned.1.call-start = ((), (), s32[]{:S(2)}) async-start(), calls=%async_computation.1 | async-start | bytes 16777216 | tf_op jit(solution)/shard_map/psum | solution.py:9
  11.7 271.5 %copy-start.1 = (f32[2048]{0:T(1024)S(1)}, f32[2048]{0:T(1024)}, u32[]{:S(2)}) copy-start(f32[2048]{0:T(1024)} %param.4) | copy-start | bytes 24580
  11.7 363.2 %reduce-scatter.2.cloned.1.call-start = ((), (), s32[]{:S(2)}) async-start(), calls=%async_computation.2 | async-start | bytes 6291456 | tf_op jit(solution)/shard_map/reduce_scatter | solution.py:24
  283.2 17.6 %slice-start = ((s8[8388608]{0:T(1024)(128)(4,1)}), s8[4194304]{0:T(1024)(128)(4,1)S(1)}, s32[]{:S(2)}) async-start(s8[8388608]{0:T(1024)(128)(4,1)} %bitcast.44), calls=%async_computation.4 | async-start | bytes 8388608
  293.1 7.8 %slice-start.1 = ((s8[8388608]{0:T(1024)(128)(4,1)}), s8[4194304]{0:T(1024)(128)(4,1)S(1)}, s32[]{:S(2)}) async-start(s8[8388608]{0:T(1024)(128)(4,1)} %bitcast.44), calls=%async_computation.5 | async-start | bytes 8388608
  293.1 7.8 %copy-start = (bf16[2,1024,2048]{2,1,0:T(8,128)(2,1)S(1)}, bf16[2,1024,2048]{2,1,0:T(8,128)(2,1)}, u32[]{:S(2)}) copy-start(bf16[2,1024,2048]{2,1,0:T(8,128)(2,1)} %multiply_convert_fusion) | copy-start | bytes 25165828
  320.4 113.4 %all-gather.2.cloned.1.call-start = ((), (), s32[]{:S(2)}) async-start(), calls=%async_computation.3 | async-start | bytes 6291456 | tf_op jit(solution)/shard_map/all_gather | solution.py:27
Sparse Core Ops, SparseCore 0:
  11.9 271.2 all-reduce.1
  320.6 54.2 reduce-scatter.1
  377.1 56.7 all-gather.1
where the time goes:
time: 454 us; the launch traced here: 451 us
  waiting for transfers between devices  385 us (85%)
  matrix products  24.9 us (5%)
  other arithmetic  20.9 us (5%)
  between operations  14.5 us (3%)
  local copies, waits for them, and re-layouts  6.2 us (1%)
    psum x1, waiting for transfers between devices, from_root(): return lax.psum(kept, axis)  271 us
    all_gather x1, waiting for transfers between devices, body(): gathered = lax.all_gather(kernel_rows, 'gvec', axis=1, tiled=True)  59 us
    reduce_scatter x1, waiting for transfers between devices, body(): lax.psum_scatter(partial_terms.astype(jnp.bfloat16), 'gvec', scatter_dime...  54.4 us
    dot_general x4, matrix products, contract(): lax.dot_general(left, right, (((1,), (1,)), ((), ())), preferred_element_...  24.9 us
    convert_element_type x1, other arithmetic, body(): (block.astype(jnp.float32) * coulomb[None, None, :]).astype(jnp.bfloat16)  9.89 us
  transfers between devices with their start and end apart: 3, of which 3 were waited for; matrix products, arithmetic and copies ran while one was open for 0% of the time, Pallas kernels for 0%

commit v1 on v0

v1 whole, which is shorter than its diff:
```python
import functools

import jax
import jax.numpy as jnp
from jax import lax
from jax.experimental import pallas as pl
from jax.experimental.pallas import tpu as pltpu
from jax.sharding import PartitionSpec as P

MESH = pl.DeviceIdType.MESH
CHUNK = 32
GROUP = 128
HOP = 2
OTHER = 4
SETTLE = 2


def contract(left, right):
    return lax.dot_general(
        left, right, (((1,), (1,)), ((), ())), preferred_element_type=jnp.float32
    )


def kernel(
    n, ng, index_ref, pd_ref, coulomb_ref, rows_ref, mirror_ref,
    near, up, down, final, other, weighted, weighted_other, term, arrived,
    near_send, near_recv, share_send, share_recv, up_send, up_recv,
    down_send, down_recv, cross_send, cross_recv, term_send, term_recv,
):
    r, t, y = lax.axis_index("rows"), lax.axis_index("trans"), lax.axis_index("gvec")
    line = n // 2
    z, x = t // 2, t % 2
    chunks = near.shape[0]
    half = chunks * CHUNK
    groups = term.shape[0]
    depth = pd_ref.shape[2]
    per = GROUP // CHUNK
    tiles = pd_ref.shape[1]
    across = {"trans": 2 * z + 1 - x}
    above, below = {"trans": t + 2}, {"trans": t - 2}
    sibling = {"rows": 1 - r}

    barrier = pltpu.get_barrier_semaphore()

    def greet(device):
        pl.semaphore_signal(barrier, inc=1, device_id=device, device_id_type=MESH)

    greet(across)
    greet(sibling)
    for p in range(1, ng):
        greet({"gvec": (y + p) % ng})

    @pl.when(z > 0)
    def _():
        greet(below)

    @pl.when(z < line - 1)
    def _():
        greet(above)

    pl.semaphore_wait(
        barrier, 1 + ng + jnp.where(z > 0, 1, 0) + jnp.where(z < line - 1, 1, 0)
    )

    def remote(source, target, send, recv, device):
        return pltpu.make_async_remote_copy(
            src_ref=source, dst_ref=target, send_sem=send, recv_sem=recv,
            device_id=device, device_id_type=MESH,
        )

    def own_rows(side, c):
        return pl.ds(pl.multiple_of(side * half + c * CHUNK, CHUNK), CHUNK)

    def near_copy(c):
        return remote(
            pd_ref.at[r, own_rows(1 - x, c), :], near.at[c, r],
            near_send.at[c], near_recv.at[c], across,
        )

    def share_copy(c):
        return remote(near.at[c, r], near.at[c, r], share_send.at[c], share_recv.at[c], sibling)

    def up_copy(c):
        return remote(up.at[c], up.at[c], up_send.at[c], up_recv.at[c], above)

    def down_copy(c):
        return remote(down.at[c], down.at[c], down_send.at[c], down_recv.at[c], below)

    def cross_copy(c):
        return remote(final.at[c], other.at[c], cross_send.at[c], cross_recv.at[c], across)

    def term_copy(g, p):
        return remote(
            term.at[g], arrived.at[p - 1, g], term_send.at[p - 1, g], term_recv.at[p - 1, g],
            {"gvec": (y + p) % ng},
        )

    source = index_ref[0]
    source_z, source_x = source // 2, source % 2
    here = source_z == z
    mine = source_x == x

    def start_near(c, carry):
        near_copy(c).start()
        return carry

    lax.fori_loop(0, chunks, start_near, 0)
    near_copy(0).wait_recv()
    share_copy(0).start()

    def base(c):
        return jnp.where(mine, pd_ref[:, own_rows(x, c), :], near[c])

    def weigh(held, c, target):
        at = pl.multiple_of((c % per) * CHUNK, CHUNK)
        scale = coulomb_ref[...]
        real = (held[0].astype(jnp.float32) * scale).astype(jnp.bfloat16)
        imag = (held[1].astype(jnp.float32) * scale).astype(jnp.bfloat16)
        target[pl.ds(at, CHUNK), :depth] = real
        target[pl.ds(at, CHUNK), depth:] = imag
        target[pl.ds(GROUP + at, CHUNK), :depth] = -imag
        target[pl.ds(GROUP + at, CHUNK), depth:] = real

    def multiply(g, target):
        tile = min(512, tiles)

        def one(i, carry):
            at = pl.ds(pl.multiple_of(i * tile, tile), tile)
            total = contract(pd_ref[0, at, :], target[:, :depth])
            total = total + contract(pd_ref[1, at, :], target[:, depth:])
            term[g, at, :] = total.astype(jnp.bfloat16)
            return carry

        lax.fori_loop(0, tiles // tile, one, 0)
        for p in range(1, ng):
            term_copy(g, p).start()

    def settle(g):
        for p in range(1, ng):
            term_copy(g, p).wait_recv()
        tile = min(256, tiles)

        def one(i, carry):
            at = pl.ds(pl.multiple_of(i * tile, tile), tile)
            total = term[g, at, :].astype(jnp.float32)
            for p in range(1, ng):
                total = total + arrived[p - 1, g, at, :].astype(jnp.float32)
            columns = pl.ds(pl.multiple_of(g * GROUP, GROUP), GROUP)
            summed = total.astype(jnp.bfloat16)
            mirror_ref[0, at, columns] = summed[:, :GROUP]
            mirror_ref[1, at, columns] = -summed[:, GROUP:]

            @pl.when(g // (groups // ng) == y)
            def _():
                to = pl.ds(pl.multiple_of((g % (groups // ng)) * GROUP, GROUP), GROUP)
                rows_ref[0, to, at] = summed[:, :GROUP].T
                rows_ref[1, to, at] = summed[:, GROUP:].T

            return carry

        lax.fori_loop(0, tiles // tile, one, 0)

    side_groups = groups // 2
    lag = (line - 1) * HOP

    def step(s, carry):
        @pl.when(s + 1 < chunks)
        def _():
            near_copy(s + 1).wait_recv()
            share_copy(s + 1).start()

        @pl.when(s < chunks)
        def _():
            share_copy(s).wait_recv()

        u = s - z * HOP

        @pl.when((u >= 0) & (u < chunks))
        def _():
            @pl.when(z == 0)
            def _():
                up[u] = base(u)

            @pl.when(z > 0)
            def _():
                up_copy(u).wait_recv()
                up[u] = jnp.where(here, base(u), up[u])

            @pl.when(z < line - 1)
            def _():
                up_copy(u).start()

        d = s - (line - 1 - z) * HOP

        @pl.when((d >= 0) & (d < chunks))
        def _():
            @pl.when(z == line - 1)
            def _():
                down[d] = base(d)

            @pl.when(z < line - 1)
            def _():
                down_copy(d).wait_recv()
                down[d] = jnp.where(here, base(d), down[d])

            @pl.when(z > 0)
            def _():
                down_copy(d).start()

        f = s - lag

        @pl.when((f >= 0) & (f < chunks))
        def _():
            final[f] = jnp.where(source_z <= z, up[f], down[f])
            cross_copy(f).start()
            weigh(final[f], f, weighted)

            @pl.when(f % per == per - 1)
            def _():
                multiply(x * side_groups + f // per, weighted)

        o = f - OTHER

        @pl.when((o >= 0) & (o < chunks))
        def _():
            cross_copy(o).wait_recv()
            weigh(other[o], o, weighted_other)

            @pl.when(o % per == per - 1)
            def _():
                multiply((1 - x) * side_groups + o // per, weighted_other)

        a = f - SETTLE

        @pl.when((a >= 0) & (a < chunks) & (a % per == per - 1))
        def _():
            settle(x * side_groups + a // per)

        b = o - SETTLE

        @pl.when((b >= 0) & (b < chunks) & (b % per == per - 1))
        def _():
            settle((1 - x) * side_groups + b // per)

        return carry

    lax.fori_loop(0, chunks + lag + OTHER + SETTLE, step, 0)

    def drain(c, carry):
        near_copy(c).wait_send()
        share_copy(c).wait_send()
        cross_copy(c).wait_send()

        @pl.when(z < line - 1)
        def _():
            up_copy(c).wait_send()

        @pl.when(z > 0)
        def _():
            down_copy(c).wait_send()

        return carry

    lax.fori_loop(0, chunks, drain, 0)

    def drain_terms(g, carry):
        for p in range(1, ng):
            term_copy(g, p).wait_send()
        return carry

    lax.fori_loop(0, groups, drain_terms, 0)


def solution(mesh):
    n, ng = mesh.shape["trans"], mesh.shape["gvec"]

    def body(pair_density, coulomb, block_index):
        _, rows, depth = pair_density.shape
        chunks = rows // 2 // CHUNK
        groups = rows // GROUP
        slots = pltpu.VMEM((chunks, 2, CHUNK, depth), jnp.bfloat16)
        sems = pltpu.SemaphoreType.DMA((chunks,))
        vmem = pl.BlockSpec(memory_space=pltpu.VMEM)
        return pl.pallas_call(
            functools.partial(kernel, n, ng),
            out_shape=(
                jax.ShapeDtypeStruct((2, rows // ng, rows), jnp.bfloat16),
                jax.ShapeDtypeStruct((2, rows, rows), jnp.bfloat16),
            ),
            in_specs=[pl.BlockSpec(memory_space=pltpu.SMEM), vmem, vmem],
            out_specs=(vmem, vmem),
            scratch_shapes=[slots] * 5
            + [pltpu.VMEM((2 * GROUP, 2 * depth), jnp.bfloat16)] * 2
            + [
                pltpu.VMEM((groups, rows, 2 * GROUP), jnp.bfloat16),
                pltpu.VMEM((ng - 1, groups, rows, 2 * GROUP), jnp.bfloat16),
            ]
            + [sems] * 10
            + [pltpu.SemaphoreType.DMA((ng - 1, groups))] * 2,
            compiler_params=pltpu.CompilerParams(
                collective_id=0, has_side_effects=True, vmem_limit_bytes=58 * 2**20
            ),
            cost_estimate=pl.CostEstimate(
                flops=8 * rows * rows * depth, bytes_accessed=28 * 2**20, transcendentals=0
            ),
        )(block_index, pair_density, coulomb[None, :])

    placed = (P(None, "trans", "gvec"), P("gvec"), P("rows"))
    return jax.shard_map(
        body,
        mesh=mesh,
        in_specs=placed,
        out_specs=(P(None, ("rows", "gvec"), "trans"), P(None, "trans", "rows")),
        check_vma=False,
    )
```

time: 454 us -> 177 us (0.39)
  waiting for transfers between devices: 385 us -> 0 us
  Pallas kernels: 0 us -> 170 us
  matrix products: 24.9 us -> 0 us
  other arithmetic: 20.9 us -> 0 us
  between operations: 14.5 us -> 1.29 us
    psum x1 -> x0, waiting for transfers between devices: 271 us -> none  [from_root(): return lax.psum(kept, axis)]
    pallas_call x0 -> x1, Pallas kernels: none -> 170 us  [body(): pl.pallas_call(functools.partial(kernel, n, ng), out_shape=(jax.ShapeDtyp...]
    all_gather x1 -> x0, waiting for transfers between devices: 59 us -> none  [body(): gathered = lax.all_gather(kernel_rows, 'gvec', axis=1, tiled=True)]
    reduce_scatter x1 -> x0, waiting for transfers between devices: 54.4 us -> none  [body(): lax.psum_scatter(partial_terms.astype(jnp.bfloat16), 'gvec', scatter_dime...]
    dot_general x4 -> x0, matrix products: 24.9 us -> none  [contract(): lax.dot_general(left, right, (((1,), (1,)), ((), ())), preferred_element_...]
    convert_element_type x1 -> x0, other arithmetic: 9.89 us -> none  [body(): (block.astype(jnp.float32) * coulomb[None, None, :]).astype(jnp.bfloat16)]
    another operation x3 -> x0, other arithmetic: 7.18 us -> none  [the longest x2 4.8 us: body(): mirrored = jnp.stack([gathered[0].T, -gathered[1].T])]
  transfers between devices with their start and end apart: 3 -> 0, of which waited for: 3 -> 0; matrix products, arithmetic and copies ran while one was open for 0% -> 0% of each run, Pallas kernels for 0% -> 0%
where the time goes in v1:
time: 177 us
  Pallas kernels  170 us (96%)
  local copies, waits for them, and re-layouts  5.25 us (3%)
    pallas_call x1, Pallas kernels, body(): pl.pallas_call(functools.partial(kernel, n, ng), out_shape=(jax.ShapeDtyp...  170 us
    unnamed x4, local copies, waits for them, and re-layouts  5.25 us

profile of v1, /device:TPU:18, one launch (start us, length us, event | category | flops | bytes accessed | tf_op | source)
XLA Modules:
  0.0 176.7 jit_solution(9424983887062692336)
XLA Ops:
  1.3 170.1 %shard_map.50 = (bf16[2,512,1024]{2,1,0:T(8,128)(2,1)}, bf16[2,1024,1024]{2,1,0:T(8,128)(2,1)}) custom-call(s32[1]{0:T(128)S(6)} %copy.7.index_ref, bf16[2,1024,2048]{2,1,0:T(8,128)(2,1)} %pd_ref.1, f32[1,2048]{1,0:T(1,128)} %bitcast.1), custom_call_target="tpu_custom_call" | custom-call | flops 17179869184 | bytes 29360128 | tf_op jit(solution)/shard_map/pallas_call | solution.py:284
  171.4 0.0 copy-start
  171.4 3.2 %copy.8 = bf16[2,512,1024]{2,1,0:T(8,128)(2,1)} copy(bf16[2,512,1024]{2,1,0:T(8,128)(2,1)} %get-tuple-element.4) | data formatting | bytes 4194304
  174.6 0.0 copy-done
  174.7 2.0 %copy.9 = bf16[2,1024,1024]{2,1,0:T(8,128)(2,1)} copy(bf16[2,1024,1024]{2,1,0:T(8,128)(2,1)S(1)} %copy-done) | data formatting | bytes 8388608
Async XLA Ops:
  171.4 3.2 %copy-start = (bf16[2,1024,1024]{2,1,0:T(8,128)(2,1)S(1)}, bf16[2,1024,1024]{2,1,0:T(8,128)(2,1)}, u32[]{:S(2)}) copy-start(bf16[2,1024,1024]{2,1,0:T(8,128)(2,1)} %get-tuple-element.5) | copy-start | bytes 12582916

commit v2 on v1

--- a/solution.py
+++ b/solution.py
@@ -8,11 +8,12 @@
 from jax.sharding import PartitionSpec as P
 
 MESH = pl.DeviceIdType.MESH
-CHUNK = 32
+CHUNK = 16
 GROUP = 128
+PART = 64
 HOP = 2
-OTHER = 4
-SETTLE = 2
+OTHER = 12
+SETTLE = 3
 
 
 def contract(left, right):
@@ -22,10 +23,11 @@
 
 
 def kernel(
-    n, ng, index_ref, pd_ref, coulomb_ref, rows_ref, mirror_ref,
-    near, up, down, final, other, weighted, weighted_other, term, arrived,
+    n, ng, index_ref, pd_in, coulomb_ref, rows_out, mirror_out,
+    pd_ref, rows_ref, mirror_ref, near, up, down, final, other, weighted, weighted_other, term, arrived,
     near_send, near_recv, share_send, share_recv, up_send, up_recv,
     down_send, down_recv, cross_send, cross_recv, term_send, term_recv,
+    load_sem, rows_sem, mirror_sem,
 ):
     r, t, y = lax.axis_index("rows"), lax.axis_index("trans"), lax.axis_index("gvec")
     line = n // 2
@@ -39,6 +41,8 @@
     across = {"trans": 2 * z + 1 - x}
     above, below = {"trans": t + 2}, {"trans": t - 2}
     sibling = {"rows": 1 - r}
+    load = pltpu.make_async_copy(pd_in, pd_ref, load_sem)
+    load.start()
 
     barrier = pltpu.get_barrier_semaphore()
 
@@ -73,7 +77,7 @@
 
     def near_copy(c):
         return remote(
-            pd_ref.at[r, own_rows(1 - x, c), :], near.at[c, r],
+            pd_in.at[r, own_rows(1 - x, c), :], near.at[c, r],
             near_send.at[c], near_recv.at[c], across,
         )
 
@@ -89,10 +93,25 @@
     def cross_copy(c):
         return remote(final.at[c], other.at[c], cross_send.at[c], cross_recv.at[c], across)
 
-    def term_copy(g, p):
+    def term_copy(g, part, p):
+        wide = pl.ds(pl.multiple_of(part * 2 * PART, 2 * PART), 2 * PART)
         return remote(
-            term.at[g], arrived.at[p - 1, g], term_send.at[p - 1, g], term_recv.at[p - 1, g],
+            term.at[g, :, wide], arrived.at[p - 1, g, :, wide],
+            term_send.at[p - 1, g, part], term_recv.at[p - 1, g, part],
             {"gvec": (y + p) % ng},
+        )
+
+    def columns(g):
+        return pl.ds(pl.multiple_of(g * GROUP, GROUP), GROUP)
+
+    def mirror_copy(g):
+        return pltpu.make_async_copy(
+            mirror_ref.at[:, :, columns(g)], mirror_out.at[:, :, columns(g)], mirror_sem.at[g]
+        )
+
+    def rows_copy(g):
+        return pltpu.make_async_copy(
+            rows_ref.at[:, columns(g), :], rows_out.at[:, columns(g), :], rows_sem.at[g]
         )
 
     source = index_ref[0]
@@ -105,6 +124,7 @@
         return carry
 
     lax.fori_loop(0, chunks, start_near, 0)
+    load.wait()
     near_copy(0).wait_recv()
     share_copy(0).start()
 
@@ -112,53 +132,64 @@
         return jnp.where(mine, pd_ref[:, own_rows(x, c), :], near[c])
 
     def weigh(held, c, target):
-        at = pl.multiple_of((c % per) * CHUNK, CHUNK)
+        row = (c % per) * CHUNK
+        at = pl.multiple_of((row // PART) * 2 * PART + row % PART, CHUNK)
         scale = coulomb_ref[...]
         real = (held[0].astype(jnp.float32) * scale).astype(jnp.bfloat16)
         imag = (held[1].astype(jnp.float32) * scale).astype(jnp.bfloat16)
         target[pl.ds(at, CHUNK), :depth] = real
         target[pl.ds(at, CHUNK), depth:] = imag
-        target[pl.ds(GROUP + at, CHUNK), :depth] = -imag
-        target[pl.ds(GROUP + at, CHUNK), depth:] = real
-
-    def multiply(g, target):
+        target[pl.ds(PART + at, CHUNK), :depth] = -imag
+        target[pl.ds(PART + at, CHUNK), depth:] = real
+
+    def multiply(g, parts, target):
         tile = min(512, tiles)
+        lanes = 2 * PART * len(parts)
+        first = parts[0] * 2 * PART
 
         def one(i, carry):
             at = pl.ds(pl.multiple_of(i * tile, tile), tile)
-            total = contract(pd_ref[0, at, :], target[:, :depth])
-            total = total + contract(pd_ref[1, at, :], target[:, depth:])
-            term[g, at, :] = total.astype(jnp.bfloat16)
+            total = contract(pd_ref[0, at, :], target[first:first + lanes, :depth])
+            total = total + contract(pd_ref[1, at, :], target[first:first + lanes, depth:])
+            term[g, at, first:first + lanes] = total.astype(jnp.bfloat16)
             return carry
 
         lax.fori_loop(0, tiles // tile, one, 0)
-        for p in range(1, ng):
-            term_copy(g, p).start()
+        for part in parts:
+            for p in range(1, ng):
+                term_copy(g, part, p).start()
 
     def settle(g):
-        for p in range(1, ng):
-            term_copy(g, p).wait_recv()
+        for part in range(GROUP // PART):
+            for p in range(1, ng):
+                term_copy(g, part, p).wait_recv()
         tile = min(256, tiles)
+        share = groups // ng
 
         def one(i, carry):
             at = pl.ds(pl.multiple_of(i * tile, tile), tile)
             total = term[g, at, :].astype(jnp.float32)
             for p in range(1, ng):
                 total = total + arrived[p - 1, g, at, :].astype(jnp.float32)
-            columns = pl.ds(pl.multiple_of(g * GROUP, GROUP), GROUP)
             summed = total.astype(jnp.bfloat16)
-            mirror_ref[0, at, columns] = summed[:, :GROUP]
-            mirror_ref[1, at, columns] = -summed[:, GROUP:]
-
-            @pl.when(g // (groups // ng) == y)
-            def _():
-                to = pl.ds(pl.multiple_of((g % (groups // ng)) * GROUP, GROUP), GROUP)
-                rows_ref[0, to, at] = summed[:, :GROUP].T
-                rows_ref[1, to, at] = summed[:, GROUP:].T
+            real = jnp.concatenate([summed[:, :PART], summed[:, 2 * PART:3 * PART]], axis=1)
+            imag = jnp.concatenate([summed[:, PART:2 * PART], summed[:, 3 * PART:]], axis=1)
+            mirror_ref[0, at, columns(g)] = real
+            mirror_ref[1, at, columns(g)] = -imag
+
+            @pl.when(g // share == y)
+            def _():
+                rows_ref[0, columns(g % share), at] = real.T
+                rows_ref[1, columns(g % share), at] = imag.T
 
             return carry
 
         lax.fori_loop(0, tiles // tile, one, 0)
+        mirror_copy(g).start()
+
+        @pl.when(g // share == y)
+        def _():
+            rows_copy(g % share).start()
 
     side_groups = groups // 2
     lag = (line - 1) * HOP
@@ -217,7 +248,7 @@
 
             @pl.when(f % per == per - 1)
             def _():
-                multiply(x * side_groups + f // per, weighted)
+                multiply(x * side_groups + f // per, (0, 1), weighted)
 
         o = f - OTHER
 
@@ -226,9 +257,10 @@
             cross_copy(o).wait_recv()
             weigh(other[o], o, weighted_other)
 
-            @pl.when(o % per == per - 1)
-            def _():
-                multiply((1 - x) * side_groups + o // per, weighted_other)
+            for part in range(GROUP // PART):
+                @pl.when(o % per == (part + 1) * (PART // CHUNK) - 1)
+                def _(part=part):
+                    multiply((1 - x) * side_groups + o // per, (part,), weighted_other)
 
         a = f - SETTLE
 
@@ -264,11 +296,19 @@
     lax.fori_loop(0, chunks, drain, 0)
 
     def drain_terms(g, carry):
-        for p in range(1, ng):
-            term_copy(g, p).wait_send()
+        for part in range(GROUP // PART):
+            for p in range(1, ng):
+                term_copy(g, part, p).wait_send()
+        mirror_copy(g).wait()
         return carry
 
     lax.fori_loop(0, groups, drain_terms, 0)
+
+    def drain_rows(g, carry):
+        rows_copy(g).wait()
+        return carry
+
+    lax.fori_loop(0, groups // ng, drain_rows, 0)
 
 
 def solution(mesh):
@@ -281,22 +321,33 @@
         slots = pltpu.VMEM((chunks, 2, CHUNK, depth), jnp.bfloat16)
         sems = pltpu.SemaphoreType.DMA((chunks,))
         vmem = pl.BlockSpec(memory_space=pltpu.VMEM)
+        hbm = pl.BlockSpec(memory_space=pl.ANY)
         return pl.pallas_call(
             functools.partial(kernel, n, ng),
             out_shape=(
                 jax.ShapeDtypeStruct((2, rows // ng, rows), jnp.bfloat16),
                 jax.ShapeDtypeStruct((2, rows, rows), jnp.bfloat16),
             ),
-            in_specs=[pl.BlockSpec(memory_space=pltpu.SMEM), vmem, vmem],
-            out_specs=(vmem, vmem),
-            scratch_shapes=[slots] * 5
+            in_specs=[pl.BlockSpec(memory_space=pltpu.SMEM), hbm, vmem],
+            out_specs=(hbm, hbm),
+            scratch_shapes=[
+                pltpu.VMEM(pair_density.shape, jnp.bfloat16),
+                pltpu.VMEM((2, rows // ng, rows), jnp.bfloat16),
+                pltpu.VMEM((2, rows, rows), jnp.bfloat16),
+            ]
+            + [slots] * 5
             + [pltpu.VMEM((2 * GROUP, 2 * depth), jnp.bfloat16)] * 2
             + [
                 pltpu.VMEM((groups, rows, 2 * GROUP), jnp.bfloat16),
                 pltpu.VMEM((ng - 1, groups, rows, 2 * GROUP), jnp.bfloat16),
             ]
             + [sems] * 10
-            + [pltpu.SemaphoreType.DMA((ng - 1, groups))] * 2,
+            + [pltpu.SemaphoreType.DMA((ng - 1, groups, GROUP // PART))] * 2
+            + [
+                pltpu.SemaphoreType.DMA,
+                pltpu.SemaphoreType.DMA((groups // ng,)),
+                pltpu.SemaphoreType.DMA((groups,)),
+            ],
             compiler_params=pltpu.CompilerParams(
                 collective_id=0, has_side_effects=True, vmem_limit_bytes=58 * 2**20
             ),

time: 177 us -> 175 us (0.989)
  Pallas kernels: 170 us -> 166 us
    pallas_call x1, Pallas kernels: 170 us -> 166 us  [body(): pl.pallas_call(functools.partial(kernel, n, ng), out_shape=(jax.ShapeDtyp...]
where the time goes in v2:
time: 175 us; the launch traced here: 173 us
  Pallas kernels  166 us (95%)
  local copies, waits for them, and re-layouts  5.25 us (3%)
    pallas_call x1, Pallas kernels, body(): pl.pallas_call(functools.partial(kernel, n, ng), out_shape=(jax.ShapeDtyp...  166 us
    unnamed x4, local copies, waits for them, and re-layouts  5.25 us

profile of v2, /device:TPU:18, one launch (start us, length us, event | category | flops | bytes accessed | tf_op | source)
XLA Modules:
  0.0 173.0 jit_solution(12319971657006656582)
XLA Ops:
  1.3 166.4 %shard_map.50 = (bf16[2,512,1024]{2,1,0:T(8,128)(2,1)}, bf16[2,1024,1024]{2,1,0:T(8,128)(2,1)}) custom-call(s32[1]{0:T(128)S(6)} %copy.7.index_ref, bf16[2,1024,2048]{2,1,0:T(8,128)(2,1)} %pd_in.1, f32[1,2048]{1,0:T(1,128)} %bitcast.1), custom_call_target="tpu_custom_call" | custom-call | flops 17179869184 | bytes 29360128 | tf_op jit(solution)/shard_map/pallas_call | solution.py:325
  167.7 0.0 copy-start
  167.7 3.2 %copy.8 = bf16[2,512,1024]{2,1,0:T(8,128)(2,1)} copy(bf16[2,512,1024]{2,1,0:T(8,128)(2,1)} %get-tuple-element.4) | data formatting | bytes 4194304
  171.0 0.0 copy-done
  171.0 2.0 %copy.9 = bf16[2,1024,1024]{2,1,0:T(8,128)(2,1)} copy(bf16[2,1024,1024]{2,1,0:T(8,128)(2,1)S(1)} %copy-done) | data formatting | bytes 8388608
Async XLA Ops:
  167.7 3.2 %copy-start = (bf16[2,1024,1024]{2,1,0:T(8,128)(2,1)S(1)}, bf16[2,1024,1024]{2,1,0:T(8,128)(2,1)}, u32[]{:S(2)}) copy-start(bf16[2,1024,1024]{2,1,0:T(8,128)(2,1)} %get-tuple-element.5) | copy-start | bytes 12582916

commit v3 on v2

--- a/solution.py
+++ b/solution.py
@@ -14,6 +14,7 @@
 HOP = 2
 OTHER = 12
 SETTLE = 3
+TILE = 256
 
 
 def contract(left, right):
@@ -37,7 +38,7 @@
     groups = term.shape[0]
     depth = pd_ref.shape[2]
     per = GROUP // CHUNK
-    tiles = pd_ref.shape[1]
+    tiles = pd_ref.shape[1] // TILE
     across = {"trans": 2 * z + 1 - x}
     above, below = {"trans": t + 2}, {"trans": t - 2}
     sibling = {"rows": 1 - r}
@@ -93,11 +94,17 @@
     def cross_copy(c):
         return remote(final.at[c], other.at[c], cross_send.at[c], cross_recv.at[c], across)
 
-    def term_copy(g, part, p):
-        wide = pl.ds(pl.multiple_of(part * 2 * PART, 2 * PART), 2 * PART)
+    def rows_of(i):
+        return pl.ds(pl.multiple_of(i * TILE, TILE), TILE)
+
+    def term_copy(g, i, part, p):
+        if part is None:
+            lanes, slot = pl.ds(0, 2 * GROUP), 0
+        else:
+            lanes, slot = pl.ds(pl.multiple_of(part * 2 * PART, 2 * PART), 2 * PART), part
         return remote(
-            term.at[g, :, wide], arrived.at[p - 1, g, :, wide],
-            term_send.at[p - 1, g, part], term_recv.at[p - 1, g, part],
+            term.at[g, rows_of(i), lanes], arrived.at[p - 1, g, rows_of(i), lanes],
+            term_send.at[p - 1, g, i, slot], term_recv.at[p - 1, g, i, slot],
             {"gvec": (y + p) % ng},
         )
 
@@ -131,68 +138,55 @@
     def base(c):
         return jnp.where(mine, pd_ref[:, own_rows(x, c), :], near[c])
 
-    def weigh(held, c, target):
-        row = (c % per) * CHUNK
+    def weigh(held, row, slot, target):
         at = pl.multiple_of((row // PART) * 2 * PART + row % PART, CHUNK)
         scale = coulomb_ref[...]
         real = (held[0].astype(jnp.float32) * scale).astype(jnp.bfloat16)
         imag = (held[1].astype(jnp.float32) * scale).astype(jnp.bfloat16)
-        target[pl.ds(at, CHUNK), :depth] = real
-        target[pl.ds(at, CHUNK), depth:] = imag
-        target[pl.ds(PART + at, CHUNK), :depth] = -imag
-        target[pl.ds(PART + at, CHUNK), depth:] = real
-
-    def multiply(g, parts, target):
-        tile = min(512, tiles)
-        lanes = 2 * PART * len(parts)
-        first = parts[0] * 2 * PART
-
-        def one(i, carry):
-            at = pl.ds(pl.multiple_of(i * tile, tile), tile)
-            total = contract(pd_ref[0, at, :], target[first:first + lanes, :depth])
-            total = total + contract(pd_ref[1, at, :], target[first:first + lanes, depth:])
-            term[g, at, first:first + lanes] = total.astype(jnp.bfloat16)
-            return carry
-
-        lax.fori_loop(0, tiles // tile, one, 0)
+        target[slot, pl.ds(at, CHUNK), :depth] = real
+        target[slot, pl.ds(at, CHUNK), depth:] = imag
+        target[slot, pl.ds(PART + at, CHUNK), :depth] = -imag
+        target[slot, pl.ds(PART + at, CHUNK), depth:] = real
+
+    def multiply(i, left):
+        total = contract(pd_ref[0, rows_of(i), :], left[:, :depth])
+        total = total + contract(pd_ref[1, rows_of(i), :], left[:, depth:])
+        return total.astype(jnp.bfloat16)
+
+    share = groups // ng
+
+    def settle(g, i, parts):
         for part in parts:
             for p in range(1, ng):
-                term_copy(g, part, p).start()
-
-    def settle(g):
-        for part in range(GROUP // PART):
-            for p in range(1, ng):
-                term_copy(g, part, p).wait_recv()
-        tile = min(256, tiles)
-        share = groups // ng
-
-        def one(i, carry):
-            at = pl.ds(pl.multiple_of(i * tile, tile), tile)
-            total = term[g, at, :].astype(jnp.float32)
-            for p in range(1, ng):
-                total = total + arrived[p - 1, g, at, :].astype(jnp.float32)
-            summed = total.astype(jnp.bfloat16)
-            real = jnp.concatenate([summed[:, :PART], summed[:, 2 * PART:3 * PART]], axis=1)
-            imag = jnp.concatenate([summed[:, PART:2 * PART], summed[:, 3 * PART:]], axis=1)
-            mirror_ref[0, at, columns(g)] = real
-            mirror_ref[1, at, columns(g)] = -imag
+                term_copy(g, i, part, p).wait_recv()
+        at = rows_of(i)
+        total = term[g, at, :].astype(jnp.float32)
+        for p in range(1, ng):
+            total = total + arrived[p - 1, g, at, :].astype(jnp.float32)
+        summed = total.astype(jnp.bfloat16)
+        real = jnp.concatenate([summed[:, :PART], summed[:, 2 * PART:3 * PART]], axis=1)
+        imag = jnp.concatenate([summed[:, PART:2 * PART], summed[:, 3 * PART:]], axis=1)
+        mirror_ref[0, at, columns(g)] = real
+        mirror_ref[1, at, columns(g)] = -imag
+
+        @pl.when(g // share == y)
+        def _():
+            rows_ref[0, columns(g % share), at] = real.T
+            rows_ref[1, columns(g % share), at] = imag.T
+
+        @pl.when(i == tiles - 1)
+        def _():
+            mirror_copy(g).start()
 
             @pl.when(g // share == y)
             def _():
-                rows_ref[0, columns(g % share), at] = real.T
-                rows_ref[1, columns(g % share), at] = imag.T
-
-            return carry
-
-        lax.fori_loop(0, tiles // tile, one, 0)
-        mirror_copy(g).start()
-
-        @pl.when(g // share == y)
-        def _():
-            rows_copy(g % share).start()
+                rows_copy(g % share).start()
 
     side_groups = groups // 2
     lag = (line - 1) * HOP
+    per_part = PART // CHUNK
+    pace = per // tiles
+    assert per_part == tiles and pace == 2
 
     def step(s, carry):
         @pl.when(s + 1 < chunks)
@@ -244,39 +238,55 @@
         def _():
             final[f] = jnp.where(source_z <= z, up[f], down[f])
             cross_copy(f).start()
-            weigh(final[f], f, weighted)
-
-            @pl.when(f % per == per - 1)
-            def _():
-                multiply(x * side_groups + f // per, (0, 1), weighted)
+            weigh(final[f], (f % per) * CHUNK, (f // per) % 2, weighted)
 
         o = f - OTHER
 
         @pl.when((o >= 0) & (o < chunks))
         def _():
             cross_copy(o).wait_recv()
-            weigh(other[o], o, weighted_other)
-
-            for part in range(GROUP // PART):
-                @pl.when(o % per == (part + 1) * (PART // CHUNK) - 1)
+            weigh(other[o], (o % per_part) * CHUNK, (o // per_part) % 2, weighted_other)
+
+        m = f - per
+
+        @pl.when((m >= 0) & (m < chunks) & (m % pace == 0))
+        def _():
+            q, i = m // per, (m % per) // pace
+            g = x * side_groups + q
+            term[g, rows_of(i), :] = multiply(i, weighted.at[q % 2])
+            for p in range(1, ng):
+                term_copy(g, i, None, p).start()
+
+        m = o - per_part
+
+        @pl.when((m >= 0) & (m < chunks))
+        def _():
+            q, i = m // per_part, m % per_part
+            g = (1 - x) * side_groups + q // 2
+            for part in range(2):
+                @pl.when(q % 2 == part)
                 def _(part=part):
-                    multiply((1 - x) * side_groups + o // per, (part,), weighted_other)
-
-        a = f - SETTLE
-
-        @pl.when((a >= 0) & (a < chunks) & (a % per == per - 1))
-        def _():
-            settle(x * side_groups + a // per)
-
-        b = o - SETTLE
-
-        @pl.when((b >= 0) & (b < chunks) & (b % per == per - 1))
-        def _():
-            settle((1 - x) * side_groups + b // per)
-
-        return carry
-
-    lax.fori_loop(0, chunks + lag + OTHER + SETTLE, step, 0)
+                    term[g, rows_of(i), part * 2 * PART:(part + 1) * 2 * PART] = multiply(
+                        i, weighted_other.at[part]
+                    )
+                    for p in range(1, ng):
+                        term_copy(g, i, part, p).start()
+
+        a = f - per - SETTLE
+
+        @pl.when((a >= 0) & (a < chunks) & (a % pace == 0))
+        def _():
+            settle(x * side_groups + a // per, (a % per) // pace, (None,))
+
+        b = o - per - SETTLE
+
+        @pl.when((b >= 0) & (b < chunks) & (b % per < tiles))
+        def _():
+            settle((1 - x) * side_groups + b // per, b % per, (0, 1))
+
+        return carry
+
+    lax.fori_loop(0, chunks + lag + OTHER + per + SETTLE, step, 0)
 
     def drain(c, carry):
         near_copy(c).wait_send()
@@ -296,13 +306,19 @@
     lax.fori_loop(0, chunks, drain, 0)
 
     def drain_terms(g, carry):
-        for part in range(GROUP // PART):
+        def drain_tile(i, inner):
             for p in range(1, ng):
-                term_copy(g, part, p).wait_send()
+                term_copy(x * side_groups + g, i, None, p).wait_send()
+                for part in range(2):
+                    term_copy((1 - x) * side_groups + g, i, part, p).wait_send()
+            return inner
+
+        lax.fori_loop(0, tiles, drain_tile, 0)
         mirror_copy(g).wait()
-        return carry
-
-    lax.fori_loop(0, groups, drain_terms, 0)
+        mirror_copy(side_groups + g).wait()
+        return carry
+
+    lax.fori_loop(0, side_groups, drain_terms, 0)
 
     def drain_rows(g, carry):
         rows_copy(g).wait()
@@ -336,13 +352,16 @@
                 pltpu.VMEM((2, rows, rows), jnp.bfloat16),
             ]
             + [slots] * 5
-            + [pltpu.VMEM((2 * GROUP, 2 * depth), jnp.bfloat16)] * 2
+            + [
+                pltpu.VMEM((2, 2 * GROUP, 2 * depth), jnp.bfloat16),
+                pltpu.VMEM((2, 2 * PART, 2 * depth), jnp.bfloat16),
+            ]
             + [
                 pltpu.VMEM((groups, rows, 2 * GROUP), jnp.bfloat16),
                 pltpu.VMEM((ng - 1, groups, rows, 2 * GROUP), jnp.bfloat16),
             ]
             + [sems] * 10
-            + [pltpu.SemaphoreType.DMA((ng - 1, groups, GROUP // PART))] * 2
+            + [pltpu.SemaphoreType.DMA((ng - 1, groups, rows // TILE, GROUP // PART))] * 2
             + [
                 pltpu.SemaphoreType.DMA,
                 pltpu.SemaphoreType.DMA((groups // ng,)),

time: 175 us -> 163 us (0.931)
  Pallas kernels: 166 us -> 155 us
    pallas_call x1, Pallas kernels: 166 us -> 155 us  [body(): pl.pallas_call(functools.partial(kernel, n, ng), out_shape=(jax.ShapeDtyp...]
where the time goes in v3:
time: 163 us; the launch traced here: 162 us
  Pallas kernels  155 us (95%)
  local copies, waits for them, and re-layouts  5.25 us (3%)
    pallas_call x1, Pallas kernels, body(): pl.pallas_call(functools.partial(kernel, n, ng), out_shape=(jax.ShapeDtyp...  155 us
    unnamed x4, local copies, waits for them, and re-layouts  5.25 us

profile of v3, /device:TPU:18, one launch (start us, length us, event | category | flops | bytes accessed | tf_op | source)
XLA Modules:
  0.0 161.8 jit_solution(1440534775242772098)
XLA Ops:
  1.3 155.2 %shard_map.50 = (bf16[2,512,1024]{2,1,0:T(8,128)(2,1)}, bf16[2,1024,1024]{2,1,0:T(8,128)(2,1)}) custom-call(s32[1]{0:T(128)S(6)} %copy.7.index_ref, bf16[2,1024,2048]{2,1,0:T(8,128)(2,1)} %pd_in.1, f32[1,2048]{1,0:T(1,128)} %bitcast.1), custom_call_target="tpu_custom_call" | custom-call | flops 17179869184 | bytes 29360128 | tf_op jit(solution)/shard_map/pallas_call | solution.py:341
  156.5 0.0 copy-start
  156.5 3.2 %copy.8 = bf16[2,512,1024]{2,1,0:T(8,128)(2,1)} copy(bf16[2,512,1024]{2,1,0:T(8,128)(2,1)} %get-tuple-element.4) | data formatting | bytes 4194304
  159.8 0.0 copy-done
  159.8 2.0 %copy.9 = bf16[2,1024,1024]{2,1,0:T(8,128)(2,1)} copy(bf16[2,1024,1024]{2,1,0:T(8,128)(2,1)S(1)} %copy-done) | data formatting | bytes 8388608
Async XLA Ops:
  156.5 3.2 %copy-start = (bf16[2,1024,1024]{2,1,0:T(8,128)(2,1)S(1)}, bf16[2,1024,1024]{2,1,0:T(8,128)(2,1)}, u32[]{:S(2)}) copy-start(bf16[2,1024,1024]{2,1,0:T(8,128)(2,1)} %get-tuple-element.5) | copy-start | bytes 12582916

commit v4 on v3

--- a/solution.py
+++ b/solution.py
@@ -12,9 +12,10 @@
 GROUP = 128
 PART = 64
 HOP = 2
-OTHER = 12
+OTHER = 6
 SETTLE = 3
 TILE = 256
+AHEAD = 6
 
 
 def contract(left, right):
@@ -130,7 +131,7 @@
         near_copy(c).start()
         return carry
 
-    lax.fori_loop(0, chunks, start_near, 0)
+    lax.fori_loop(0, AHEAD, start_near, 0)
     load.wait()
     near_copy(0).wait_recv()
     share_copy(0).start()
@@ -189,6 +190,13 @@
     assert per_part == tiles and pace == 2
 
     def step(s, carry):
+        for extra in range(2):
+            c = AHEAD + 2 * s + extra
+
+            @pl.when(c < chunks)
+            def _(c=c):
+                near_copy(c).start()
+
         @pl.when(s + 1 < chunks)
         def _():
             near_copy(s + 1).wait_recv()

time: 163 us -> 167 us (1.025)
  Pallas kernels: 155 us -> 158 us
    pallas_call x1, Pallas kernels: 155 us -> 158 us  [body(): pl.pallas_call(functools.partial(kernel, n, ng), out_shape=(jax.ShapeDtyp...]
where the time goes in v4:
time: 167 us; the launch traced here: 164 us
  Pallas kernels  158 us (95%)
  local copies, waits for them, and re-layouts  5.25 us (3%)
    pallas_call x1, Pallas kernels, body(): pl.pallas_call(functools.partial(kernel, n, ng), out_shape=(jax.ShapeDtyp...  158 us
    unnamed x4, local copies, waits for them, and re-layouts  5.25 us

profile of v4, /device:TPU:18, one launch (start us, length us, event | category | flops | bytes accessed | tf_op | source)
XLA Modules:
  0.0 164.3 jit_solution(16191829908973023106)
XLA Ops:
  1.3 157.8 %shard_map.50 = (bf16[2,512,1024]{2,1,0:T(8,128)(2,1)}, bf16[2,1024,1024]{2,1,0:T(8,128)(2,1)}) custom-call(s32[1]{0:T(128)S(6)} %copy.7.index_ref, bf16[2,1024,2048]{2,1,0:T(8,128)(2,1)} %pd_in.1, f32[1,2048]{1,0:T(1,128)} %bitcast.1), custom_call_target="tpu_custom_call" | custom-call | flops 17179869184 | bytes 29360128 | tf_op jit(solution)/shard_map/pallas_call | solution.py:349
  159.1 0.0 copy-start
  159.1 3.2 %copy.8 = bf16[2,512,1024]{2,1,0:T(8,128)(2,1)} copy(bf16[2,512,1024]{2,1,0:T(8,128)(2,1)} %get-tuple-element.4) | data formatting | bytes 4194304
  162.3 0.0 copy-done
  162.3 2.0 %copy.9 = bf16[2,1024,1024]{2,1,0:T(8,128)(2,1)} copy(bf16[2,1024,1024]{2,1,0:T(8,128)(2,1)S(1)} %copy-done) | data formatting | bytes 8388608
Async XLA Ops:
  159.1 3.2 %copy-start = (bf16[2,1024,1024]{2,1,0:T(8,128)(2,1)S(1)}, bf16[2,1024,1024]{2,1,0:T(8,128)(2,1)}, u32[]{:S(2)}) copy-start(bf16[2,1024,1024]{2,1,0:T(8,128)(2,1)} %get-tuple-element.5) | copy-start | bytes 12582916

commit v5 on v3

--- a/solution.py
+++ b/solution.py
@@ -11,7 +11,7 @@
 CHUNK = 16
 GROUP = 128
 PART = 64
-HOP = 2
+HOP = 4
 OTHER = 12
 SETTLE = 3
 TILE = 256

time: 163 us -> 173 us (1.061)
  Pallas kernels: 155 us -> 166 us
    pallas_call x1, Pallas kernels: 155 us -> 166 us  [body(): pl.pallas_call(functools.partial(kernel, n, ng), out_shape=(jax.ShapeDtyp...]
where the time goes in v5:
time: 173 us
  Pallas kernels  166 us (96%)
  local copies, waits for them, and re-layouts  5.25 us (3%)
    pallas_call x1, Pallas kernels, body(): pl.pallas_call(functools.partial(kernel, n, ng), out_shape=(jax.ShapeDtyp...  166 us
    unnamed x4, local copies, waits for them, and re-layouts  5.25 us

profile of v5, /device:TPU:18, one launch (start us, length us, event | category | flops | bytes accessed | tf_op | source)
XLA Modules:
  0.0 173.0 jit_solution(12714957981641392565)
XLA Ops:
  1.3 166.5 %shard_map.50 = (bf16[2,512,1024]{2,1,0:T(8,128)(2,1)}, bf16[2,1024,1024]{2,1,0:T(8,128)(2,1)}) custom-call(s32[1]{0:T(128)S(6)} %copy.7.index_ref, bf16[2,1024,2048]{2,1,0:T(8,128)(2,1)} %pd_in.1, f32[1,2048]{1,0:T(1,128)} %bitcast.1), custom_call_target="tpu_custom_call" | custom-call | flops 17179869184 | bytes 29360128 | tf_op jit(solution)/shard_map/pallas_call | solution.py:341
  167.8 0.0 copy-start
  167.8 3.2 %copy.8 = bf16[2,512,1024]{2,1,0:T(8,128)(2,1)} copy(bf16[2,512,1024]{2,1,0:T(8,128)(2,1)} %get-tuple-element.4) | data formatting | bytes 4194304
  171.0 0.0 copy-done
  171.0 2.0 %copy.9 = bf16[2,1024,1024]{2,1,0:T(8,128)(2,1)} copy(bf16[2,1024,1024]{2,1,0:T(8,128)(2,1)S(1)} %copy-done) | data formatting | bytes 8388608
Async XLA Ops:
  167.8 3.2 %copy-start = (bf16[2,1024,1024]{2,1,0:T(8,128)(2,1)S(1)}, bf16[2,1024,1024]{2,1,0:T(8,128)(2,1)}, u32[]{:S(2)}) copy-start(bf16[2,1024,1024]{2,1,0:T(8,128)(2,1)} %get-tuple-element.5) | copy-start | bytes 12582916

commit v6 on v3

--- a/solution.py
+++ b/solution.py
@@ -12,7 +12,7 @@
 GROUP = 128
 PART = 64
 HOP = 2
-OTHER = 12
+OTHER = 8
 SETTLE = 3
 TILE = 256
 

time: 163 us -> 164 us (level)
  no operation moved by 1% of the time
where the time goes in v6:
time: 164 us; the launch traced here: 161 us
  Pallas kernels  155 us (95%)
  local copies, waits for them, and re-layouts  5.25 us (3%)
    pallas_call x1, Pallas kernels, body(): pl.pallas_call(functools.partial(kernel, n, ng), out_shape=(jax.ShapeDtyp...  155 us
    unnamed x4, local copies, waits for them, and re-layouts  5.25 us

profile of v6, /device:TPU:18, one launch (start us, length us, event | category | flops | bytes accessed | tf_op | source)
XLA Modules:
  0.0 161.4 jit_solution(2255664950677358642)
XLA Ops:
  1.3 154.9 %shard_map.50 = (bf16[2,512,1024]{2,1,0:T(8,128)(2,1)}, bf16[2,1024,1024]{2,1,0:T(8,128)(2,1)}) custom-call(s32[1]{0:T(128)S(6)} %copy.7.index_ref, bf16[2,1024,2048]{2,1,0:T(8,128)(2,1)} %pd_in.1, f32[1,2048]{1,0:T(1,128)} %bitcast.1), custom_call_target="tpu_custom_call" | custom-call | flops 17179869184 | bytes 29360128 | tf_op jit(solution)/shard_map/pallas_call | solution.py:341
  156.1 0.0 copy-start
  156.2 3.2 %copy.8 = bf16[2,512,1024]{2,1,0:T(8,128)(2,1)} copy(bf16[2,512,1024]{2,1,0:T(8,128)(2,1)} %get-tuple-element.4) | data formatting | bytes 4194304
  159.4 0.0 copy-done
  159.4 2.0 %copy.9 = bf16[2,1024,1024]{2,1,0:T(8,128)(2,1)} copy(bf16[2,1024,1024]{2,1,0:T(8,128)(2,1)S(1)} %copy-done) | data formatting | bytes 8388608
Async XLA Ops:
  156.1 3.2 %copy-start = (bf16[2,1024,1024]{2,1,0:T(8,128)(2,1)S(1)}, bf16[2,1024,1024]{2,1,0:T(8,128)(2,1)}, u32[]{:S(2)}) copy-start(bf16[2,1024,1024]{2,1,0:T(8,128)(2,1)} %get-tuple-element.5) | copy-start | bytes 12582916
